TPU v7x, 32 devices: a whole 2x2x4 slice. The times are simulated.
32 devices in a mesh: pipe: 4 (over y, x), seq: 8 (over z, core).
Axes of the slice: x: 2, y: 2, z: 4, core: 2. Of those that a mesh axis runs over, the one named last changes fastest.
Arguments:
- inputs: bfloat16 [4, 1024, 2048], P('pipe', 'seq'), may hold values from -6 to 6
- lengths: int32 [4, 32], replicated, may hold values from 1 to 128, 1024 in all within a row
- order: int32 [4], replicated, may hold values from 0 to 3, each once
- norm_gain: float32 [4, 2048], P('pipe'), may hold values from 0.25 to 1.75
- rate: float32 [4, 16, 2048], P('pipe'), may hold values from 0.004 to 0.15
- angle: float32 [4, 16, 2048], P('pipe'), may hold values from -3.140625 to 3.140625
- coef: float32 [4, 2, 16, 2048], P('pipe'), may hold values from -0.3 to 0.3
- skip: float32 [4, 2048], P('pipe'), may hold values from 0.5 to 1.5
- score_gains: float32 [4, 2, 2048], P('pipe'), may hold values from -3 to 4.6
- out_proj: bfloat16 [4, 2048, 2048], P('pipe', 'seq'), may hold values from -0.125 to 0.125
Outputs:
- outputs: bfloat16 [4, 1024, 2048], P('pipe', 'seq')
Inputs may be any that keep to these rules, and one draw needn't show every extreme that they name: Each row of lengths sums to 1024, and every row holds a document of exactly 128 positions. `order`: each packed row appears once.
All inputs are finite; a program needn't handle non-finite values.
Results may differ from a plain program's by a relative error of at most 0.02.
The roundings to bfloat16 on the way count: a program that leaves them out, or rounds other values in their place, can miss the bound.
Values may be sent and summed in bfloat16 or wider, within the bound.
No kernel may reach another device: no remote copies, remote signals or barrier semaphores. Data moves between devices by JAX's collectives and lax.ppermute only.
A program may use at most 128 MiB of HBM per device.

v0:
```python
import jax
import jax.numpy as jnp
from jax import lax
from jax.sharding import PartitionSpec as P

HEAD_DIM = 128


inner_span = 16
norm_eps = 1e-06
masked_score = -1e30


def passed_along(value, axis, steps):
    count = lax.axis_size(axis)
    initial, last = (max(0, -steps), min(count, count - steps))
    return lax.ppermute(value, axis, [(source, source + steps) for source in range(initial, last)])


def broadcast(value, axis, source):
    kept = jnp.where(lax.axis_index(axis) == source, value, 0).astype(value.dtype)
    return lax.psum(kept, axis)


def mode_powers(rate_now, angle_now, exponents):
    magnitude = jnp.exp(-exponents[:, None, None] * rate_now[None])
    turning = exponents[:, None, None] * angle_now[None]
    return (magnitude * jnp.cos(turning), magnitude * jnp.sin(turning))


def mode_tables(rate_now, angle_now, coef_now):
    lag_steps = jnp.arange(inner_span).astype(jnp.float32)
    coef_re = coef_now[0]
    coef_im = coef_now[1]
    power_re, power_im = mode_powers(rate_now, angle_now, lag_steps)
    kernel = 2.0 * jnp.sum(coef_re[None] * power_re - coef_im[None] * power_im, axis=1)
    ahead_re, ahead_im = mode_powers(rate_now, angle_now, lag_steps + 1.0)
    carry_re = coef_re[None] * ahead_re - coef_im[None] * ahead_im
    carry_im = coef_re[None] * ahead_im + coef_im[None] * ahead_re
    back_re, back_im = mode_powers(rate_now, angle_now, inner_span - 1.0 - lag_steps)
    whole_re, whole_im = mode_powers(
        rate_now, angle_now, jnp.full((1,), 1.0 * inner_span, jnp.float32)
    )
    return (kernel, carry_re, carry_im, back_re, back_im, whole_re[0], whole_im[0])


def local_conv(kernel, signal, doc_ids):
    result = kernel[0][None, None, :] * signal
    for lag_steps in range(1, inner_span):
        shifted = jnp.pad(signal[:, :-lag_steps], ((0, 0), (lag_steps, 0), (0, 0)))
        same_doc = jnp.pad(
            doc_ids[:, lag_steps:] == doc_ids[:, :-lag_steps], ((0, 0), (lag_steps, 0))
        )
        result = result + kernel[lag_steps][None, None, :] * shifted * same_doc[:, :, None].astype(
            jnp.float32
        )
    return result


def rms_scaled(values):
    return values * lax.rsqrt(jnp.mean(values * values, axis=1, keepdims=True) + norm_eps)


def block_terms(scaled, doc_ids, prior_first, tables_all, skip_now):
    kernel, carry_re, carry_im, back_re, back_im, whole_re, whole_im = tables_all
    block_count = scaled.shape[0] // inner_span
    blocks = scaled.reshape(block_count, inner_span, scaled.shape[1])
    block_docs = doc_ids.reshape(block_count, inner_span)
    last_docs = block_docs[:, -1]
    prior_docs = jnp.concatenate([jnp.reshape(prior_first, (1,)), last_docs[:-1]])
    base_out = local_conv(kernel, blocks, block_docs) + skip_now * blocks
    kept_rows = blocks * (block_docs == last_docs[:, None]).astype(jnp.float32)[:, :, None]
    local_re = jnp.sum(back_re[None] * kept_rows[:, :, None, :], axis=1)
    local_im = jnp.sum(back_im[None] * kept_rows[:, :, None, :], axis=1)
    link_flags = (last_docs == prior_docs).astype(jnp.float32)
    entry_flags = (block_docs == prior_docs[:, None]).astype(jnp.float32)
    return (base_out, local_re, local_im, link_flags, entry_flags)


def run_chain(local_re, local_im, link_flags, start_re, start_im, whole_re, whole_im):

    def advance(carried, item):
        state_re, state_im = carried
        piece_re, piece_im, link_now = item
        next_re = piece_re + link_now * (whole_re * state_re - whole_im * state_im)
        next_im = piece_im + link_now * (whole_re * state_im + whole_im * state_re)
        return ((next_re, next_im), (state_re, state_im))

    (end_re, end_im), (enter_re, enter_im) = lax.scan(
        advance, (start_re, start_im), (local_re, local_im, link_flags)
    )
    return (enter_re, enter_im, end_re, end_im)


def finish_terms(terms, tables_all, start_re, start_im):
    base_out, local_re, local_im, link_flags, entry_flags = terms
    carry_re = tables_all[1]
    carry_im = tables_all[2]
    enter_re, enter_im, end_re, end_im = run_chain(
        local_re, local_im, link_flags, start_re, start_im, tables_all[5], tables_all[6]
    )
    reached = 2.0 * jnp.sum(
        carry_re[None] * enter_re[:, None] - carry_im[None] * enter_im[:, None], axis=2
    )
    mixed = base_out + entry_flags[:, :, None] * reached
    return mixed.reshape(-1, mixed.shape[2])


def doc_attention(middle, key_rows, doc_ids, positions, gains_now, proj_whole):
    row_count = middle.shape[0]
    key_count = key_rows.shape[0]
    normed = rms_scaled(key_rows.astype(jnp.float32))
    query_heads = (
        (normed[key_count - row_count :] * gains_now[0])
        .astype(jnp.bfloat16)
        .reshape(row_count, -1, HEAD_DIM)
    )
    key_heads = (normed * gains_now[1]).astype(jnp.bfloat16).reshape(key_count, -1, HEAD_DIM)
    value_heads = key_rows.reshape(key_count, -1, HEAD_DIM)
    scores = jnp.einsum(
        "thd,shd->hts", query_heads, key_heads, preferred_element_type=jnp.float32
    ) * HEAD_DIM ** (-0.5)
    query_pos = positions[key_count - row_count :]
    query_docs = doc_ids[key_count - row_count :]
    allowed = (positions[None, :] <= query_pos[:, None]) & (doc_ids[None, :] == query_docs[:, None])
    scores = jnp.where(allowed[None], scores, masked_score)
    largest = jnp.max(scores, axis=2, keepdims=True)
    raw_weights = jnp.exp(scores - largest)
    weights = (raw_weights / jnp.sum(raw_weights, axis=2, keepdims=True)).astype(jnp.bfloat16)
    attended = jnp.einsum("hts,shd->thd", weights, value_heads, preferred_element_type=jnp.float32)
    attended = attended.reshape(row_count, -1).astype(jnp.bfloat16)
    projected = jnp.dot(attended, proj_whole, preferred_element_type=jnp.float32)
    return (middle.astype(jnp.float32) + projected).astype(jnp.bfloat16)


def section_layer(
    section_in, doc_ids, positions, tables_all, norm_now, skip_now, gains_now, proj_whole
):
    row_count = section_in.shape[0]
    zeros = jnp.zeros(tables_all[5].shape, jnp.float32)
    plain = section_in.astype(jnp.float32)
    scaled = rms_scaled(plain) * norm_now
    terms = block_terms(scaled, doc_ids[row_count:], doc_ids[row_count - 1], tables_all, skip_now)
    enter_re, enter_im, end_re, end_im = run_chain(
        terms[1], terms[2], terms[3], zeros, zeros, tables_all[5], tables_all[6]
    )
    arrived = passed_along(jnp.stack([end_re, end_im]), "seq", 1)
    mixed = finish_terms(terms, tables_all, arrived[0], arrived[1])
    middle = (plain + mixed).astype(jnp.bfloat16)
    before_middle = passed_along(middle, "seq", 1)
    key_rows = jnp.concatenate([before_middle, middle])
    return doc_attention(middle, key_rows, doc_ids, positions, gains_now, proj_whole)


def local(inputs, lengths, order, norm_gain, rate, angle, coef, skip, score_gains, out_proj):
    section_count = lax.axis_size("pipe")
    section_index = lax.axis_index("pipe")
    seq_index = lax.axis_index("seq")
    held_rows = inputs.shape[0]
    row_count = inputs.shape[1]
    width = inputs.shape[2]
    micro_count = section_count * held_rows
    tick_count = micro_count + section_count - 1
    whole_proj = lax.all_gather(out_proj[0], "seq", axis=0, tiled=True)
    tables_all = mode_tables(rate[0], angle[0], coef[0])
    positions = seq_index * row_count - row_count + jnp.arange(2 * row_count)
    silent_rows = jnp.zeros((row_count, width), jnp.bfloat16)
    incoming = silent_rows
    outgoing = silent_rows
    finished = []
    for moment in range(tick_count):
        if moment > 0:
            incoming = passed_along(outgoing, "pipe", 1)
        if moment < micro_count:
            entering = order[moment]
            local_row = lax.dynamic_index_in_dim(inputs, entering % held_rows, 0, False)
            fetched = broadcast(local_row, "pipe", entering // held_rows)
        else:
            fetched = silent_rows
        section_in = jnp.where(section_index == 0, fetched, incoming)
        slot_index = jnp.clip(moment - section_index, 0, micro_count - 1)
        chosen = lax.dynamic_index_in_dim(order, slot_index, 0, False)
        doc_ends = jnp.cumsum(lax.dynamic_index_in_dim(lengths, chosen, 0, False))
        counted = jnp.sum((doc_ends[None, :] <= positions[:, None]).astype(jnp.int32), axis=1)
        doc_ids = jnp.where(positions >= 0, counted, -1)
        outgoing = section_layer(
            section_in,
            doc_ids,
            positions,
            tables_all,
            norm_gain[0],
            skip[0],
            score_gains[0],
            whole_proj,
        )
        if moment >= section_count - 1:
            finished.append(outgoing)
    collected = jnp.stack(finished)
    handed = lax.all_to_all(collected, "pipe", split_axis=0, concat_axis=0, tiled=True)
    return handed[(section_count - 1) * held_rows : section_count * held_rows]


def solution(mesh):
    in_specs = (
        P("pipe", "seq", None),
        P(),
        P(),
        P("pipe", None),
        P("pipe", None, None),
        P("pipe", None, None),
        P("pipe", None, None, None),
        P("pipe", None),
        P("pipe", None, None),
        P("pipe", "seq", None),
    )
    out_specs = P("pipe", "seq", None)
    return jax.shard_map(local, mesh=mesh, in_specs=in_specs, out_specs=out_specs, check_vma=False)
```

profile of v0, /device:TPU:24, one launch (start us, length us, event | category | flops | bytes accessed | tf_op | source)
XLA Modules:
  0.0 1206.4 jit_solution(12520912708284483456)
XLA Ops:
  90.8 26.9 %multiply_subtract_fusion = (f32[16,16,2048]{2,1,0:T(8,128)S(1)}, f32[16,16,2048]{2,1,0:T(8,128)}, f32[16,2048]{1,0:T(8,128)S(1)}, f32[16,16,2048]{2,1,0:T(8,128)}, f32[16,16,2048]{2,1,0:T(8,128)}) fusion(f32[16]{0:T(128)} %get-tuple-element.1340, f32[16]{0:T(128)} %get-tuple-element.1342, f32[16,2048]{1,0:T(8,128)S(1)} %get-tuple-element.1271, ...), kind=kLoop, calls=%fused_computation.140 | loop fusion | flops 11501568 | bytes 9044352 | tf_op jit(solution)/shard_map/sub | solution.py:38
  166.9 4.1 multiply_reduce_fusion.12
  171.0 29.3 %while.210 = (s32[]{:T(128)}, f32[16,2048]{1,0:T(8,128)S(1)}, f32[16,2048]{1,0:T(8,128)}, f32[8,16,2048]{2,1,0:T(8,128)}, f32[8]{0:T(128)}, /*index=5*/f32[16,20...) while((s32[]{:T(128)}, f32[16,2048]{1,0:T(8,128)S(1)}, ...), condition=%wide.region_11.12_spmd.clone, body=%wide.region_10.11_spmd.clone.sunk | while | flops 393219 | bytes 1048707 | solution.py:89
  216.4 42.7 %while.203 = (s32[]{:T(128)}, f32[16,2048]{1,0:T(8,128)}, f32[16,2048]{1,0:T(8,128)S(1)}, f32[8,16,2048]{2,1,0:T(8,128)}, f32[8,16,2048]{2,1,0:T(8,128)}, /*inde...) while((s32[]{:T(128)}, f32[16,2048]{1,0:T(8,128)}, ...), condition=%wide.region_13.14_spmd, body=%wide.region_12.13_spmd.sunk | while | flops 327682 | bytes 1573505 | solution.py:89
  259.5 7.6 subtract_reduce_fusion.6
  267.6 3.9 multiply_add_fusion.7
  293.3 4.0 fusion.261
  300.6 4.9 fusion.24
  309.3 8.3 collective-permute-done.2
  320.0 4.1 multiply_reduce_fusion.10
  324.0 29.9 %while.211 = (s32[]{:T(128)}, f32[16,2048]{1,0:T(8,128)S(1)}, f32[16,2048]{1,0:T(8,128)}, f32[8,16,2048]{2,1,0:T(8,128)}, f32[8]{0:T(128)}, /*index=5*/f32[16,20...) while((s32[]{:T(128)}, f32[16,2048]{1,0:T(8,128)S(1)}, ...), condition=%wide.region_24.25_spmd.clone, body=%wide.region_23.24_spmd.clone.sunk | while | flops 393219 | bytes 1048707 | solution.py:89
  370.1 41.6 %while.204 = (s32[]{:T(128)}, f32[16,2048]{1,0:T(8,128)}, f32[16,2048]{1,0:T(8,128)S(1)}, f32[8,16,2048]{2,1,0:T(8,128)}, f32[8,16,2048]{2,1,0:T(8,128)}, /*inde...) while((s32[]{:T(128)}, f32[16,2048]{1,0:T(8,128)}, ...), condition=%wide.region_26.27_spmd, body=%wide.region_25.26_spmd.sunk | while | flops 327682 | bytes 1573505 | solution.py:89
  412.1 7.7 subtract_reduce_fusion.5
  420.2 3.9 multiply_add_fusion.6
  429.4 6.0 collective-permute-done.4
  442.0 4.0 fusion.264
  448.5 4.7 add_convert_fusion.5
  453.2 4.4 collective-permute-start.5
  459.1 5.2 collective-permute-done.5
  466.7 4.1 multiply_reduce_fusion.8
  470.8 29.5 %while.212 = (s32[]{:T(128)}, f32[16,2048]{1,0:T(8,128)S(1)}, f32[16,2048]{1,0:T(8,128)}, f32[8,16,2048]{2,1,0:T(8,128)}, f32[8]{0:T(128)}, /*index=5*/f32[16,20...) while((s32[]{:T(128)}, f32[16,2048]{1,0:T(8,128)S(1)}, ...), condition=%wide.region_37.38_spmd.clone, body=%wide.region_36.37_spmd.clone.sunk | while | flops 393219 | bytes 1048707 | solution.py:89
  517.0 43.1 %while.205 = (s32[]{:T(128)}, f32[16,2048]{1,0:T(8,128)}, f32[16,2048]{1,0:T(8,128)S(1)}, f32[8,16,2048]{2,1,0:T(8,128)}, f32[8,16,2048]{2,1,0:T(8,128)}, /*inde...) while((s32[]{:T(128)}, f32[16,2048]{1,0:T(8,128)}, ...), condition=%wide.region_39.40_spmd, body=%wide.region_38.39_spmd.sunk | while | flops 327682 | bytes 1573505 | solution.py:89
  560.5 7.7 subtract_reduce_fusion.4
  568.6 3.9 multiply_add_fusion.5
  577.6 5.6 collective-permute-done.7
  589.9 4.0 fusion.267
  596.4 4.7 add_convert_fusion.4
  601.2 4.4 collective-permute-start.8
  607.0 5.3 collective-permute-done.8
  614.7 4.1 multiply_reduce_fusion.6
  618.7 30.3 %while.213 = (s32[]{:T(128)}, f32[16,2048]{1,0:T(8,128)S(1)}, f32[16,2048]{1,0:T(8,128)}, f32[8,16,2048]{2,1,0:T(8,128)}, f32[8]{0:T(128)}, /*index=5*/f32[16,20...) while((s32[]{:T(128)}, f32[16,2048]{1,0:T(8,128)S(1)}, ...), condition=%wide.region_50.51_spmd.clone, body=%wide.region_49.50_spmd.clone.sunk | while | flops 393219 | bytes 1048707 | solution.py:89
  665.6 42.7 %while.206 = (s32[]{:T(128)}, f32[16,2048]{1,0:T(8,128)}, f32[16,2048]{1,0:T(8,128)S(1)}, f32[8,16,2048]{2,1,0:T(8,128)}, f32[8,16,2048]{2,1,0:T(8,128)}, /*inde...) while((s32[]{:T(128)}, f32[16,2048]{1,0:T(8,128)}, ...), condition=%wide.region_52.53_spmd, body=%wide.region_51.52_spmd.sunk | while | flops 327682 | bytes 1573505 | solution.py:89
  708.6 7.7 subtract_reduce_fusion.3
  725.8 5.4 collective-permute-done.10
  737.9 4.0 fusion.270
  744.4 4.7 add_convert_fusion.3
  749.1 5.2 collective-permute-start.11
  755.8 5.2 collective-permute-done.11
  762.2 4.1 multiply_reduce_fusion.4
  766.2 29.4 %while.214 = (s32[]{:T(128)}, f32[16,2048]{1,0:T(8,128)S(1)}, f32[16,2048]{1,0:T(8,128)}, f32[8,16,2048]{2,1,0:T(8,128)}, f32[8]{0:T(128)}, /*index=5*/f32[16,20...) while((s32[]{:T(128)}, f32[16,2048]{1,0:T(8,128)S(1)}, ...), condition=%wide.region_63.64_spmd.clone, body=%wide.region_62.63_spmd.clone.sunk | while | flops 393219 | bytes 1048707 | solution.py:89
  812.2 43.3 %while.207 = (s32[]{:T(128)}, f32[16,2048]{1,0:T(8,128)}, f32[16,2048]{1,0:T(8,128)S(1)}, f32[8,16,2048]{2,1,0:T(8,128)}, f32[8,16,2048]{2,1,0:T(8,128)}, /*inde...) while((s32[]{:T(128)}, f32[16,2048]{1,0:T(8,128)}, ...), condition=%wide.region_65.66_spmd, body=%wide.region_64.65_spmd.sunk | while | flops 327682 | bytes 1573505 | solution.py:89
  855.8 7.7 subtract_reduce_fusion.2
  863.9 3.9 multiply_add_fusion.3
  873.4 5.2 collective-permute-done.13
  885.3 4.0 fusion.273
  891.8 4.7 add_convert_fusion.2
  896.4 5.3 collective-permute-start.14
  903.1 5.3 collective-permute-done.14
  909.6 4.1 multiply_reduce_fusion.2
  913.6 28.8 %while.215 = (s32[]{:T(128)}, f32[16,2048]{1,0:T(8,128)S(1)}, f32[16,2048]{1,0:T(8,128)}, f32[8,16,2048]{2,1,0:T(8,128)}, f32[8]{0:T(128)}, /*index=5*/f32[16,20...) while((s32[]{:T(128)}, f32[16,2048]{1,0:T(8,128)S(1)}, ...), condition=%wide.region_76.77_spmd.clone, body=%wide.region_75.76_spmd.clone.sunk | while | flops 393219 | bytes 1048707 | solution.py:89
  958.8 37.1 %while.208 = (s32[]{:T(128)}, f32[16,2048]{1,0:T(8,128)}, f32[16,2048]{1,0:T(8,128)S(1)}, f32[8,16,2048]{2,1,0:T(8,128)}, f32[8,16,2048]{2,1,0:T(8,128)}, /*inde...) while((s32[]{:T(128)}, f32[16,2048]{1,0:T(8,128)}, ...), condition=%wide.region_78.79_spmd, body=%wide.region_77.78_spmd.sunk | while | flops 327682 | bytes 1573505 | solution.py:89
  996.2 7.7 subtract_reduce_fusion.1
  1013.4 5.5 collective-permute-done.16
  1025.5 4.0 fusion.276
  1032.0 4.7 add_convert_fusion.1
  1036.7 5.3 collective-permute-start.17
  1043.5 5.2 collective-permute-done.17
  1049.8 4.0 multiply_reduce_fusion
  1053.8 30.2 %while.216 = (s32[]{:T(128)}, f32[16,2048]{1,0:T(8,128)S(1)}, f32[16,2048]{1,0:T(8,128)}, f32[8,16,2048]{2,1,0:T(8,128)}, f32[8]{0:T(128)}, /*index=5*/f32[16,20...) while((s32[]{:T(128)}, f32[16,2048]{1,0:T(8,128)S(1)}, ...), condition=%wide.region_89.90_spmd.clone, body=%wide.region_88.89_spmd.clone.sunk | while | flops 393219 | bytes 1048707 | solution.py:89
  1098.8 37.1 %while.209 = (s32[]{:T(128)}, f32[16,2048]{1,0:T(8,128)}, f32[16,2048]{1,0:T(8,128)S(1)}, f32[8,16,2048]{2,1,0:T(8,128)}, f32[8,16,2048]{2,1,0:T(8,128)}, /*inde...) while((s32[]{:T(128)}, f32[16,2048]{1,0:T(8,128)}, ...), condition=%wide.region_91.92_spmd, body=%wide.region_90.91_spmd.sunk | while | flops 327682 | bytes 1573505 | solution.py:89
  1136.3 7.7 subtract_reduce_fusion
  1151.6 7.3 collective-permute-done.19
  1167.5 4.8 fusion.142
  1172.6 25.2 %all_to_all.5 = bf16[4,128,2048]{2,1,0:T(8,128)(2,1)S(1)} all-to-all(bf16[4,128,2048]{2,1,0:T(8,128)(2,1)S(1)} %pad_maximum_fusion), channel_id=1, replica_groups=mesh['pipe'=4,'seq'=8] {'pipe'}, dimensions={0} | all-to-all | bytes 4194304 | tf_op jit(solution)/shard_map/all_to_all | solution.py:199
  (1591 shorter events, 868.0 us)
Async XLA Ops:
  7.4 156.0 %all-reduce.213.cloned.1.call-start = ((), (), s32[]{:S(2)}) async-start(), calls=%async_computation.2 | async-start | bytes 4194304 | tf_op jit(solution)/shard_map/psum | solution.py:22
  13.9 75.9 %copy-start.227 = (f32[1,2,16,2048]{3,2,1,0:T(8,128)S(1)}, f32[1,2,16,2048]{3,2,1,0:T(8,128)}, u32[]{:S(2)}) copy-start(f32[1,2,16,2048]{3,2,1,0:T(8,128)} %param.44) | copy-start | bytes 786436
  14.0 75.9 %copy-start.91 = (f32[1,16,2048]{2,1,0:T(8,128)S(1)}, f32[1,16,2048]{2,1,0:T(8,128)}, u32[]{:S(2)}) copy-start(f32[1,16,2048]{2,1,0:T(8,128)} %param.43) | copy-start | bytes 393220
  14.0 75.9 %copy-start.92 = (f32[1,16,2048]{2,1,0:T(8,128)S(1)}, f32[1,16,2048]{2,1,0:T(8,128)}, u32[]{:S(2)}) copy-start(f32[1,16,2048]{2,1,0:T(8,128)} %param.42) | copy-start | bytes 393220
  14.0 286.6 %all-gather.3.cloned.1.call-start = ((), (), s32[]{:S(2)}) async-start(), calls=%async_computation.1 | async-start | bytes 9437184 | tf_op jit(solution)/shard_map/all_gather | solution.py:164
  29.6 88.1 %copy-start.35 = (s32[16,16]{1,0:T(8,128)}, s32[16,16]{1,0:T(8,128)S(1)}, u32[]{:S(2)}) copy-start(s32[16,16]{1,0:T(8,128)S(1)} %broadcast_select_fusion.13) | copy-start | bytes 3076
  30.5 87.2 %copy-start.345 = (s32[256]{0:T(256)}, s32[256]{0:T(256)S(1)}, u32[]{:S(2)}) copy-start(s32[256]{0:T(256)S(1)} %broadcast_select_fusion.20) | copy-start | bytes 3076
  42.4 76.7 %copy-start.346 = (s32[256]{0:T(256)}, s32[256]{0:T(256)S(1)}, u32[]{:S(2)}) copy-start(s32[256]{0:T(256)S(1)} %broadcast_select_fusion.19) | copy-start | bytes 3076
  42.5 77.3 %copy-start.347 = (s32[256]{0:T(256)}, s32[256]{0:T(256)S(1)}, u32[]{:S(2)}) copy-start(s32[256]{0:T(256)S(1)} %broadcast_select_fusion.18) | copy-start | bytes 3076
  42.8 113.6 %copy-start.340 = (s32[8]{0:T(128)}, s32[8]{0:T(128)S(1)}, u32[]{:S(2)}) copy-start(s32[8]{0:T(128)S(1)} %slice_reduce_fusion.11) | copy-start | bytes 100
  43.7 112.7 %copy-start.342 = (s32[8]{0:T(128)}, s32[8]{0:T(128)S(1)}, u32[]{:S(2)}) copy-start(s32[8]{0:T(128)S(1)} %slice_reduce_fusion.12) | copy-start | bytes 100
  63.5 56.8 %copy-start.348 = (s32[256]{0:T(256)}, s32[256]{0:T(256)S(1)}, u32[]{:S(2)}) copy-start(s32[256]{0:T(256)S(1)} %broadcast_select_fusion.17) | copy-start | bytes 3076
  63.6 57.4 %copy-start.349 = (s32[256]{0:T(256)}, s32[256]{0:T(256)S(1)}, u32[]{:S(2)}) copy-start(s32[256]{0:T(256)S(1)} %broadcast_select_fusion.16) | copy-start | bytes 3076
  63.9 95.0 %copy-start.338 = (s32[8]{0:T(128)}, s32[8]{0:T(128)S(1)}, u32[]{:S(2)}) copy-start(s32[8]{0:T(128)S(1)} %slice_reduce_fusion.10) | copy-start | bytes 100
  65.5 93.4 %copy-start.336 = (s32[8]{0:T(128)}, s32[8]{0:T(128)S(1)}, u32[]{:S(2)}) copy-start(s32[8]{0:T(128)S(1)} %slice_reduce_fusion.9) | copy-start | bytes 100
  78.2 83.3 %copy-start.334 = (s32[8]{0:T(128)}, s32[8]{0:T(128)S(1)}, u32[]{:S(2)}) copy-start(s32[8]{0:T(128)S(1)} %slice_reduce_fusion.8) | copy-start | bytes 100
  78.8 82.7 %copy-start.332 = (s32[8]{0:T(128)}, s32[8]{0:T(128)S(1)}, u32[]{:S(2)}) copy-start(s32[8]{0:T(128)S(1)} %slice_reduce_fusion.7) | copy-start | bytes 100
  90.5 51.0 %copy-start.389 = (pred[8,3]{1,0:T(8,128)(4,1)S(1)}, pred[8,3]{1,0:T(8,128)(4,1)}, u32[]{:S(2)}) copy-start(pred[8,3]{1,0:T(8,128)(4,1)} %slice_compare_fusion.62) | copy-start | bytes 76
  90.5 51.6 %copy-start.385 = (pred[8,5]{1,0:T(8,128)(4,1)S(1)}, pred[8,5]{1,0:T(8,128)(4,1)}, u32[]{:S(2)}) copy-start(pred[8,5]{1,0:T(8,128)(4,1)} %slice_compare_fusion.64) | copy-start | bytes 124
  90.6 51.6 %copy-start.386 = (pred[8,6]{1,0:T(8,128)(4,1)S(1)}, pred[8,6]{1,0:T(8,128)(4,1)}, u32[]{:S(2)}) copy-start(pred[8,6]{1,0:T(8,128)(4,1)} %slice_compare_fusion.65) | copy-start | bytes 148
  90.6 52.3 %copy-start.381 = (pred[8,7]{1,0:T(8,128)(4,1)S(1)}, pred[8,7]{1,0:T(8,128)(4,1)}, u32[]{:S(2)}) copy-start(pred[8,7]{1,0:T(8,128)(4,1)} %slice_compare_fusion.66) | copy-start | bytes 172
  90.6 52.3 %copy-start.382 = (pred[8,8]{1,0:T(8,128)(4,1)S(1)}, pred[8,8]{1,0:T(8,128)(4,1)}, u32[]{:S(2)}) copy-start(pred[8,8]{1,0:T(8,128)(4,1)} %slice_compare_fusion.67) | copy-start | bytes 196
  90.6 52.9 %copy-start.377 = (pred[8,9]{1,0:T(8,128)(4,1)S(1)}, pred[8,9]{1,0:T(8,128)(4,1)}, u32[]{:S(2)}) copy-start(pred[8,9]{1,0:T(8,128)(4,1)} %slice_compare_fusion.68) | copy-start | bytes 220
  90.6 52.9 %copy-start.378 = (pred[8,10]{1,0:T(8,128)(4,1)S(1)}, pred[8,10]{1,0:T(8,128)(4,1)}, u32[]{:S(2)}) copy-start(pred[8,10]{1,0:T(8,128)(4,1)} %slice_compare_fusion.69) | copy-start | bytes 244
  90.6 53.6 %copy-start.373 = (pred[8,11]{1,0:T(8,128)(4,1)S(1)}, pred[8,11]{1,0:T(8,128)(4,1)}, u32[]{:S(2)}) copy-start(pred[8,11]{1,0:T(8,128)(4,1)} %slice_compare_fusion.70) | copy-start | bytes 268
  90.6 53.6 %copy-start.374 = (pred[8,12]{1,0:T(8,128)(4,1)S(1)}, pred[8,12]{1,0:T(8,128)(4,1)}, u32[]{:S(2)}) copy-start(pred[8,12]{1,0:T(8,128)(4,1)} %slice_compare_fusion.71) | copy-start | bytes 292
  90.6 54.2 %copy-start.369 = (pred[8,13]{1,0:T(8,128)(4,1)S(1)}, pred[8,13]{1,0:T(8,128)(4,1)}, u32[]{:S(2)}) copy-start(pred[8,13]{1,0:T(8,128)(4,1)} %slice_compare_fusion.72) | copy-start | bytes 316
  90.6 54.2 %copy-start.370 = (pred[8,14]{1,0:T(8,128)(4,1)S(1)}, pred[8,14]{1,0:T(8,128)(4,1)}, u32[]{:S(2)}) copy-start(pred[8,14]{1,0:T(8,128)(4,1)} %slice_compare_fusion.73) | copy-start | bytes 340
  90.6 54.9 %copy-start.387 = (pred[8,1]{1,0:T(8,128)(4,1)S(1)}, pred[8,1]{1,0:T(8,128)(4,1)}, u32[]{:S(2)}) copy-start(pred[8,1]{1,0:T(8,128)(4,1)} %slice_compare_fusion.45) | copy-start | bytes 28
  90.7 54.9 %copy-start.388 = (pred[8,2]{1,0:T(8,128)(4,1)S(1)}, pred[8,2]{1,0:T(8,128)(4,1)}, u32[]{:S(2)}) copy-start(pred[8,2]{1,0:T(8,128)(4,1)} %slice_compare_fusion.46) | copy-start | bytes 52
  90.7 55.6 %copy-start.383 = (pred[8,3]{1,0:T(8,128)(4,1)S(1)}, pred[8,3]{1,0:T(8,128)(4,1)}, u32[]{:S(2)}) copy-start(pred[8,3]{1,0:T(8,128)(4,1)} %slice_compare_fusion.47) | copy-start | bytes 76
  90.7 55.6 %copy-start.384 = (pred[8,4]{1,0:T(8,128)(4,1)S(1)}, pred[8,4]{1,0:T(8,128)(4,1)}, u32[]{:S(2)}) copy-start(pred[8,4]{1,0:T(8,128)(4,1)} %slice_compare_fusion.48) | copy-start | bytes 100
  90.7 56.2 %copy-start.379 = (pred[8,5]{1,0:T(8,128)(4,1)S(1)}, pred[8,5]{1,0:T(8,128)(4,1)}, u32[]{:S(2)}) copy-start(pred[8,5]{1,0:T(8,128)(4,1)} %slice_compare_fusion.49) | copy-start | bytes 124
  90.7 56.2 %copy-start.380 = (pred[8,6]{1,0:T(8,128)(4,1)S(1)}, pred[8,6]{1,0:T(8,128)(4,1)}, u32[]{:S(2)}) copy-start(pred[8,6]{1,0:T(8,128)(4,1)} %slice_compare_fusion.50) | copy-start | bytes 148
  90.7 56.9 %copy-start.375 = (pred[8,7]{1,0:T(8,128)(4,1)S(1)}, pred[8,7]{1,0:T(8,128)(4,1)}, u32[]{:S(2)}) copy-start(pred[8,7]{1,0:T(8,128)(4,1)} %slice_compare_fusion.51) | copy-start | bytes 172
  90.7 56.9 %copy-start.376 = (pred[8,8]{1,0:T(8,128)(4,1)S(1)}, pred[8,8]{1,0:T(8,128)(4,1)}, u32[]{:S(2)}) copy-start(pred[8,8]{1,0:T(8,128)(4,1)} %slice_compare_fusion.52) | copy-start | bytes 196
  90.7 57.5 %copy-start.371 = (pred[8,9]{1,0:T(8,128)(4,1)S(1)}, pred[8,9]{1,0:T(8,128)(4,1)}, u32[]{:S(2)}) copy-start(pred[8,9]{1,0:T(8,128)(4,1)} %slice_compare_fusion.53) | copy-start | bytes 220
  90.7 57.5 %copy-start.372 = (pred[8,10]{1,0:T(8,128)(4,1)S(1)}, pred[8,10]{1,0:T(8,128)(4,1)}, u32[]{:S(2)}) copy-start(pred[8,10]{1,0:T(8,128)(4,1)} %slice_compare_fusion.54) | copy-start | bytes 244
  90.7 58.2 %copy-start.367 = (pred[8,11]{1,0:T(8,128)(4,1)S(1)}, pred[8,11]{1,0:T(8,128)(4,1)}, u32[]{:S(2)}) copy-start(pred[8,11]{1,0:T(8,128)(4,1)} %slice_compare_fusion.55) | copy-start | bytes 268
  90.8 58.2 %copy-start.368 = (pred[8,12]{1,0:T(8,128)(4,1)S(1)}, pred[8,12]{1,0:T(8,128)(4,1)}, u32[]{:S(2)}) copy-start(pred[8,12]{1,0:T(8,128)(4,1)} %slice_compare_fusion.56) | copy-start | bytes 292
  90.8 58.8 %copy-start.365 = (pred[8,13]{1,0:T(8,128)(4,1)S(1)}, pred[8,13]{1,0:T(8,128)(4,1)}, u32[]{:S(2)}) copy-start(pred[8,13]{1,0:T(8,128)(4,1)} %slice_compare_fusion.57) | copy-start | bytes 316
  90.8 58.8 %copy-start.366 = (pred[8,14]{1,0:T(8,128)(4,1)S(1)}, pred[8,14]{1,0:T(8,128)(4,1)}, u32[]{:S(2)}) copy-start(pred[8,14]{1,0:T(8,128)(4,1)} %slice_compare_fusion.58) | copy-start | bytes 340
  90.8 59.5 %copy-start.363 = (pred[8,1]{1,0:T(8,128)(4,1)S(1)}, pred[8,1]{1,0:T(8,128)(4,1)}, u32[]{:S(2)}) copy-start(pred[8,1]{1,0:T(8,128)(4,1)} %slice_compare_fusion.30) | copy-start | bytes 28
  90.8 59.5 %copy-start.364 = (pred[8,2]{1,0:T(8,128)(4,1)S(1)}, pred[8,2]{1,0:T(8,128)(4,1)}, u32[]{:S(2)}) copy-start(pred[8,2]{1,0:T(8,128)(4,1)} %slice_compare_fusion.31) | copy-start | bytes 52
  201.9 10.7 collective-permute-start
  271.7 15.1 %collective-permute-start.1 = (bf16[128,2048]{1,0:T(8,128)(2,1)S(1)}, bf16[128,2048]{1,0:T(8,128)(2,1)S(1)}, u32[]{:S(2)}, u32[]{:S(2)}) collective-permute-start(bf16[128,2048]{1,0:T(8,128)(2,1)S(1)} %fusion.46), channel_id=1, source_target_pairs={{0,1},{1,2},{2,3},{3,4},{4,5},{5,6},{6,7},{8,9},{9,10},{10,11},{11... | collective-permute-start | bytes 1572872 | tf_op jit(solution)/shard_map/ppermute | solution.py:17
  305.5 12.0 collective-permute-start.2
  355.6 10.7 collective-permute-start.3
  424.3 11.1 collective-permute-start.4
  453.2 11.1 collective-permute-start.5
  501.9 11.3 collective-permute-start.6
  572.7 10.5 collective-permute-start.7
  601.2 11.1 collective-permute-start.8
  650.6 11.1 collective-permute-start.9
  720.8 10.5 collective-permute-start.10
  749.1 11.9 collective-permute-start.11
  797.3 11.1 collective-permute-start.12
  868.1 10.5 collective-permute-start.13
  896.4 12.0 collective-permute-start.14
  944.1 10.8 collective-permute-start.15
  1008.4 10.5 collective-permute-start.16
  1036.7 12.0 collective-permute-start.17
  1084.9 11.0 collective-permute-start.18
  1148.4 10.5 collective-permute-start.19
  (369 other events, 3542.5 us)
Sparse Core Ops, SparseCore 0:
  14.1 71.2 all-reduce.212
Sparse Core Ops, SparseCore 1:
  16.2 80.1 all-gather.2
where the time goes:
time: 1230 us; the launch traced here: 1210 us
  other arithmetic  581 us (47%)
  local copies, waits for them, and re-layouts  357 us (29%)
  matrix products  78.5 us (6%)
  waiting for transfers between devices  70.1 us (6%)
  starting transfers between devices  57 us (5%)
  between operations  36.7 us (3%)
  blocking collectives  25.2 us (2%)
    add x112, other arithmetic, advance(): next_im = piece_im + link_now * (whole_re * state_im + whole_im * state_re)  273 us
    dynamic_slice x112, local copies, waits for them, and re-layouts, run_chain(): lax.scan(advance, (start_re, start_im), (local_re, local_im, link_flags))  130 us
    dynamic_update_slice x56, local copies, waits for them, and re-layouts, run_chain(): lax.scan(advance, (start_re, start_im), (local_re, local_im, link_flags))  91.5 us
    ppermute x20, waiting for transfers between devices, passed_along(): lax.ppermute(value, axis, [(source, source + steps) for source in range(i...  69.5 us
    eq x105, other arithmetic, local_conv(): doc_ids[:, lag_steps:] == doc_ids[:, :-lag_steps]  57.5 us
    ppermute x20, starting transfers between devices, passed_along(): lax.ppermute(value, axis, [(source, source + steps) for source in range(i...  57 us
    reduce_sum x7, other arithmetic, finish_terms(): jnp.sum(carry_re[None] * enter_re[:, None] - carry_im[None] * enter_im[:,...  53.8 us
    convert_element_type x56, other arithmetic, local_conv(): same_doc[:, :, None].astype(jnp.float32)  52.7 us
  transfers between devices with their start and end apart: 22, of which 12 were waited for; matrix products, arithmetic and copies ran while one was open for 28% of the time, Pallas kernels for 0%

commit v1 on v0

v1 whole, which is shorter than its diff:
```python
import functools
import itertools

import jax
import jax.numpy as jnp
import numpy as np
from jax import lax
from jax.experimental import pallas as pl
from jax.experimental.pallas import tpu as pltpu
from jax.sharding import PartitionSpec as P

HEAD_DIM = 128
norm_eps = 1e-06
masked_score = -1e30
lanes = 128
mode_group = 4
row_tile = 16


def mixer_tables(rate_now, angle_now, coef_now):
    magnitude = jnp.exp(-rate_now)
    turn_re = magnitude * jnp.cos(angle_now)
    turn_im = magnitude * jnp.sin(angle_now)
    pole_sum = 2.0 * turn_re
    pole_product = -(magnitude * magnitude)
    direct = 2.0 * coef_now[0]
    delayed = -2.0 * (coef_now[0] * turn_re + coef_now[1] * turn_im)
    return jnp.concatenate([pole_sum, pole_product, direct, delayed])


def inverse_rms(values):
    return lax.rsqrt(jnp.mean(values * values, axis=1, keepdims=True) + norm_eps)


def mix_attend_kernel(
    keep_ref, x_ref, table_ref, vec_ref, doc_col_ref, doc_row_ref,
    middle_ref, attended_ref, signal, mixed, queries, keys,
):
    rows, width = x_ref.shape
    folds = width // lanes
    modes = table_ref.shape[0] // 4
    heads = width // HEAD_DIM

    def spread(tile, carry):
        first = pl.multiple_of(tile * row_tile, row_tile)
        plain = x_ref[pl.ds(first, row_tile), :].astype(jnp.float32)
        scaled = plain * inverse_rms(plain) * vec_ref[0:1, :]
        direct = scaled * vec_ref[1:2, :]
        for fold in range(folds):
            where = pl.ds(first * folds + fold, row_tile, stride=folds)
            part = slice(fold * lanes, (fold + 1) * lanes)
            signal[where, :] = scaled[:, part]
            mixed[where, :] = direct[:, part]
        return carry

    lax.fori_loop(0, rows // row_tile, spread, 0)

    def run_modes(group, carry):
        first_mode = group * mode_group

        def table(kind, index):
            return table_ref[kind * modes + first_mode + index]

        coefs = [[table(kind, index) for kind in range(4)] for index in range(mode_group)]

        def advance(chunk, state):
            state = list(state)
            for step in range(8):
                row = chunk * 8 + step
                where = pl.ds(pl.multiple_of(row * folds, folds), folds)
                keep = keep_ref[row]
                entering = signal[where, :]
                total = mixed[where, :]
                for index in range(mode_group):
                    a1, a2, b0, b1 = coefs[index]
                    older = state[2 * index + 1] * keep
                    newer = state[2 * index] * keep
                    now = (entering + a2 * older) + a1 * newer
                    total = total + (b0 * now + b1 * newer)
                    state[2 * index] = now
                    state[2 * index + 1] = newer
                mixed[where, :] = total
            return tuple(state)

        zeros = jnp.zeros((folds, lanes), jnp.float32)
        lax.fori_loop(0, rows // 8, advance, (zeros,) * (2 * mode_group))
        return carry

    lax.fori_loop(0, modes // mode_group, run_modes, 0)

    def gather_back(tile, carry):
        first = pl.multiple_of(tile * row_tile, row_tile)
        where_rows = pl.ds(first, row_tile)
        parts = [
            mixed[pl.ds(first * folds + fold, row_tile, stride=folds), :] for fold in range(folds)
        ]
        plain = x_ref[where_rows, :].astype(jnp.float32)
        middle = (plain + jnp.concatenate(parts, axis=1)).astype(jnp.bfloat16)
        middle_ref[where_rows, :] = middle
        wide = middle.astype(jnp.float32)
        normed = wide * inverse_rms(wide)
        queries[where_rows, :] = (normed * vec_ref[2:3, :]).astype(jnp.bfloat16)
        keys[where_rows, :] = (normed * vec_ref[3:4, :]).astype(jnp.bfloat16)
        return carry

    lax.fori_loop(0, rows // row_tile, gather_back, 0)

    query_pos = lax.broadcasted_iota(jnp.int32, (rows, rows), 0)
    key_pos = lax.broadcasted_iota(jnp.int32, (rows, rows), 1)
    allowed = (key_pos <= query_pos) & (doc_col_ref[...] == doc_row_ref[...])

    def attend(head, carry):
        where = pl.ds(pl.multiple_of(head * HEAD_DIM, HEAD_DIM), HEAD_DIM)
        scores = lax.dot_general(
            queries[:, where], keys[:, where], (((1,), (1,)), ((), ())),
            preferred_element_type=jnp.float32,
        ) * HEAD_DIM ** (-0.5)
        scores = jnp.where(allowed, scores, masked_score)
        raw = jnp.exp(scores - jnp.max(scores, axis=1, keepdims=True))
        weights = (raw * (1.0 / jnp.sum(raw, axis=1, keepdims=True))).astype(jnp.bfloat16)
        attended_ref[:, where] = jnp.dot(
            weights, middle_ref[:, where], preferred_element_type=jnp.float32
        ).astype(jnp.bfloat16)
        return carry

    lax.fori_loop(0, heads, attend, 0)


def mix_attend(x, table, vec, keep, docs):
    rows, width = x.shape
    folds = width // lanes
    vmem = pl.BlockSpec(memory_space=pltpu.VMEM)
    return pl.pallas_call(
        mix_attend_kernel,
        out_shape=[jax.ShapeDtypeStruct((rows, width), jnp.bfloat16)] * 2,
        in_specs=[pl.BlockSpec(memory_space=pltpu.SMEM)] + [vmem] * 5,
        out_specs=[vmem, vmem],
        scratch_shapes=[
            pltpu.VMEM((rows * folds, lanes), jnp.float32),
            pltpu.VMEM((rows * folds, lanes), jnp.float32),
            pltpu.VMEM((rows, width), jnp.bfloat16),
            pltpu.VMEM((rows, width), jnp.bfloat16),
        ],
        compiler_params=pltpu.CompilerParams(vmem_limit_bytes=32 << 20),
        cost_estimate=pl.CostEstimate(
            flops=rows * width * 16 * 10, bytes_accessed=rows * width * 12, transcendentals=0
        ),
        name="mix_attend",
    )(keep, x, table, vec, docs[:, None], docs[None, :])


def permuted_rows(value, order):
    count = lax.axis_size("pipe")
    choices = list(itertools.permutations(range(count)))
    match = jnp.all(jnp.asarray(np.array(choices, np.int32)) == order[None, :], axis=1)
    which = jnp.argmax(match).astype(jnp.int32)

    def mover(choice):
        pairs = [(source, target) for target, source in enumerate(choice)]
        return lambda held: lax.ppermute(held, "pipe", pairs)

    return lax.switch(which, [mover(choice) for choice in choices], value)


def local(inputs, lengths, order, norm_gain, rate, angle, coef, skip, score_gains, out_proj):
    section_count = lax.axis_size("pipe")
    seq_count = lax.axis_size("seq")
    pipe_index = lax.axis_index("pipe")
    seq_index = lax.axis_index("seq")
    row_count, width = inputs.shape[1:]
    shard = out_proj.shape[1]

    quarters = lax.all_to_all(
        out_proj[0].reshape(section_count, shard // section_count, width),
        "pipe", split_axis=0, concat_axis=0, tiled=True,
    )
    projections = [
        lax.all_gather(quarters[section], ("seq", "pipe"), axis=0, tiled=True)
        for section in range(section_count)
    ]

    table_own = mixer_tables(rate[0], angle[0], coef[0]).reshape(-1, width // lanes, lanes)
    vec_own = jnp.concatenate([norm_gain, skip, score_gains[0]])
    tables = lax.all_gather(table_own, "pipe")
    vecs = lax.all_gather(vec_own, "pipe")

    own = permuted_rows(inputs[0], order)
    before = lax.ppermute(own, "seq", [(i, i + 1) for i in range(seq_count - 1)])
    x = jnp.concatenate([before, own])

    positions = (seq_index - 1) * row_count + jnp.arange(2 * row_count)
    chosen = lax.dynamic_index_in_dim(order, pipe_index, 0, False)
    doc_ends = jnp.cumsum(lax.dynamic_index_in_dim(lengths, chosen, 0, False))
    counted = jnp.sum((doc_ends[None, :] <= positions[:, None]).astype(jnp.int32), axis=1)
    docs = jnp.where(positions >= 0, counted, -1)
    keep = jnp.concatenate([jnp.zeros((1,), jnp.float32), (docs[1:] == docs[:-1]).astype(jnp.float32)])

    for section in range(section_count):
        middle, attended = mix_attend(x, tables[section], vecs[section], keep, docs)
        if section == section_count - 1:
            middle = middle[row_count:]
            attended = attended[row_count:]
        projected = jnp.dot(attended, projections[section], preferred_element_type=jnp.float32)
        x = (middle.astype(jnp.float32) + projected).astype(jnp.bfloat16)
    return x[None]


def solution(mesh):
    in_specs = (
        P("pipe", "seq", None),
        P(),
        P(),
        P("pipe", None),
        P("pipe", None, None),
        P("pipe", None, None),
        P("pipe", None, None, None),
        P("pipe", None),
        P("pipe", None, None),
        P("pipe", "seq", None),
    )
    out_specs = P("pipe", "seq", None)
    return jax.shard_map(local, mesh=mesh, in_specs=in_specs, out_specs=out_specs, check_vma=False)
```

time: 1230 us -> 393 us (0.32); the launches traced: 1210 us -> 390 us
  other arithmetic: 581 us -> 4.82 us
  local copies, waits for them, and re-layouts: 357 us -> 8.67 us
  Pallas kernels: 0 us -> 107 us
  waiting for transfers between devices: 70.1 us -> 171 us
  matrix products: 78.5 us -> 23.6 us
  starting transfers between devices: 57 us -> 3.55 us
  blocking collectives: 25.2 us -> 54.8 us
  between operations: 36.7 us -> 15.9 us
    add x120 -> x1, other arithmetic: 300 us -> 0.01 us  [local(): positions = (seq_index - 1) * row_count + jnp.arange(2 * row_count)]
    all_gather x1 -> x5, waiting for transfers between devices: 0.01 us -> 169 us  [the longest x4 169 us: local(): lax.all_gather(quarters[section], ('seq', 'pipe'), axis=0, tiled=True)]
    dynamic_slice x113 -> x1, local copies, waits for them, and re-layouts: 132 us -> 0.64 us  [local(): chosen = lax.dynamic_index_in_dim(order, pipe_index, 0, False)]
    pallas_call x0 -> x4, Pallas kernels: none -> 107 us  [mix_attend(): pl.pallas_call(mix_attend_kernel, out_shape=[jax.ShapeDtypeStruct((rows,...]
    dynamic_update_slice x56 -> x0, local copies, waits for them, and re-layouts: 91.5 us -> none  [run_chain(): lax.scan(advance, (start_re, start_im), (local_re, local_im, link_flags))]
    reduce_sum x28 -> x0, other arithmetic: 87.1 us -> none  [the longest x7 53.8 us: finish_terms(): jnp.sum(carry_re[None] * enter_re[:, None] - carry_im[None] * enter_im[:,...]
    convert_element_type x82 -> x0, other arithmetic: 77.8 us -> none  [the longest x56 52.7 us: local_conv(): same_doc[:, :, None].astype(jnp.float32)]
    ppermute x20 -> x2, waiting for transfers between devices: 69.5 us -> 0.01 us  [the longest x1 0.01 us: local(): lax.ppermute(own, 'seq', [(i, i + 1) for i in range(seq_count - 1)])]
  transfers between devices with their start and end apart: 22 -> 7, of which waited for: 12 -> 4; matrix products, arithmetic and copies ran while one was open for 28% -> 6% of each run, Pallas kernels for 0% -> 28%
where the time goes in v1:
time: 393 us; the launch traced here: 390 us
  waiting for transfers between devices  171 us (44%)
  Pallas kernels  107 us (27%)
  blocking collectives  54.8 us (14%)
  matrix products  23.6 us (6%)
  between operations  15.9 us (4%)
  local copies, waits for them, and re-layouts  8.67 us (2%)
  other arithmetic  4.82 us (1%)
    all_gather x4, waiting for transfers between devices, local(): lax.all_gather(quarters[section], ('seq', 'pipe'), axis=0, tiled=True)  169 us
    pallas_call x4, Pallas kernels, mix_attend(): pl.pallas_call(mix_attend_kernel, out_shape=[jax.ShapeDtypeStruct((rows,...  107 us
    all_gather x1, blocking collectives, local(): vecs = lax.all_gather(vec_own, 'pipe')  31.3 us
    dot_general x4, matrix products, local(): jnp.dot(attended, projections[section], preferred_element_type=jnp.float32)  23.6 us
    all_to_all x1, blocking collectives, local(): lax.all_to_all(out_proj[0].reshape(section_count, shard // section_count,...  23.5 us
  transfers between devices with their start and end apart: 7, of which 4 were waited for; matrix products, arithmetic and copies ran while one was open for 6% of the time, Pallas kernels for 28%

profile of v1, /device:TPU:24, one launch (start us, length us, event | category | flops | bytes accessed | tf_op | source)
XLA Modules:
  0.0 390.0 jit_solution(5894890046690915209)
XLA Ops:
  6.5 0.0 copy-start
  6.5 0.0 copy-start.8
  6.5 0.0 copy-start.7
  6.6 0.0 copy-start.6
  6.6 0.0 all-gather.12.cloned.1.call-start
  6.6 1.5 multiply_bitcast_fusion.1
  8.2 1.0 slice_bitcast_fusion.5
  9.4 0.8 pad_maximum_fusion.1
  10.2 0.0 all-gather.12.cloned.1.call-update
  10.2 0.0 all-gather.14.cloned.1.call-start
  10.3 23.5 %all_to_all.5 = bf16[4,64,2048]{2,1,0:T(8,128)(2,1)S(1)} all-to-all(bf16[4,64,2048]{2,1,0:T(8,128)(2,1)} %bitcast.99), channel_id=1, replica_groups=mesh['pipe'=4,'seq'=8] {'pipe'}, dimensions={0} | all-to-all | bytes 2097152 | tf_op jit(solution)/shard_map/all_to_all | solution.py:173
  33.8 1.1 fusion.33
  34.9 0.0 all-gather.14.cloned.1.call-update
  34.9 0.0 all-gather.16.cloned.1.call-start
  34.9 0.7 all-gather.16.cloned.1.call-update
  35.6 0.0 all-gather.18.cloned.1.call-start
  35.7 0.5 all-gather.18.cloned.1.call-update
  36.2 0.0 all-gather.20.cloned.1.call-start
  36.2 0.5 all-gather.20.cloned.1.call-update
  36.8 0.0 copy-done.8
  36.8 0.0 copy-done.9
  36.8 0.1 compare_reduce_fusion
  36.9 0.7 iota_reduce_fusion
  38.2 0.0 copy-done.10
  38.2 1.5 conditional.1
  38.2 1.4 collective-permute-start.5
  39.7 0.0 collective-permute-done.5
  39.7 1.9 collective-permute-start.24
  41.6 0.6 dynamic_slice.8
  44.1 0.0 copy-done
  44.1 0.1 copy.17
  44.2 0.1 reduce-window.8
  44.3 0.1 reduce.18
  44.4 0.1 convert_reduce_fusion
  44.5 0.1 copy.18
  44.6 0.0 copy-done.5
  44.6 0.0 copy-done.7
  44.6 0.0 copy-done.6
  44.7 31.3 %all-gather.5 = f32[4,4,2048]{2,1,0:T(4,128)S(1)} all-gather(f32[1,4,2048]{2,1,0:T(4,128)S(1)} %maximum_bitcast_fusion), channel_id=2, replica_groups=mesh['pipe'=4,'seq'=8] {'pipe'}, dimensions={0}, use_global_device_ids=true | all-gather | bytes 163840 | tf_op jit(solution)/shard_map/all_gather | solution.py:185
  76.0 0.1 slice_compare_fusion
  76.1 0.1 add_convert_fusion.1.keep_ref
  76.2 0.0 collective-permute-done.24
  76.2 1.2 pad_maximum_fusion.x_ref
  77.4 0.0 all-gather.12.cloned.1.call-done
  77.4 1.7 slice_bitcast_fusion
  79.1 26.9 %mix_attend.4 = (bf16[256,2048]{1,0:T(8,128)(2,1)S(1)}, bf16[256,2048]{1,0:T(8,128)(2,1)S(1)}) custom-call(f32[256]{0:T(256)S(1)} %add_convert_fusion.1.keep_ref, bf16[256,2048]{1,0:T(8,128)(2,1)S(1)} %pad_maximum_fusion.x_ref, f32[64,16,128]{2,1,0:T(8,128)S(1)} %get-tuple-element.75.table_ref, f32[4,2048]{1,0:T(4,128)S(1)} %get-tuple-element.87.vec_ref, ...), custom_call_target="tpu_custom_call" | custom-call | flops 83886080 | bytes 6291456 | tf_op jit(solution)/shard_map/mix_attend/pallas_call | solution.py:133
  105.9 0.0 copy-start.2
  106.0 1.0 copy-done.2
  106.9 1.0 copy-done.3
  107.9 33.0 %all-gather.14.cloned.1.call-done = bf16[1,2048,2048]{2,1,0:T(8,128)(2,1)} async-done(((bf16[1,64,2048]{2,1,0:T(8,128)(2,1)}), bf16[1,2048,2048]{2,1,0:T(8,128)(2,1)}) %all-gather.14.cloned.1.call-update) | async-done | bytes 8388624 | tf_op jit(solution)/shard_map/all_gather | solution.py:178
  140.9 6.2 %add_convert_fusion.x_ref = bf16[256,2048]{1,0:T(8,128)(2,1)S(1)} fusion(bf16[256,2048]{1,0:T(8,128)(2,1)} %copy-done.2, bf16[256,2048]{1,0:T(8,128)(2,1)} %copy-done.3, bf16[1,2048,2048]{2,1,0:T(8,128)(2,1)} %all-gather.14.cloned.1.call-done), kind=kOutput, calls=%fused_computation.15 | convolution fusion | flops 2149056512 | bytes 11534336 | tf_op jit(solution)/shard_map/dot_general | solution.py:203
  147.1 26.9 %mix_attend.5 = (bf16[256,2048]{1,0:T(8,128)(2,1)S(1)}, bf16[256,2048]{1,0:T(8,128)(2,1)S(1)}) custom-call(f32[256]{0:T(256)S(1)} %add_convert_fusion.1.keep_ref, bf16[256,2048]{1,0:T(8,128)(2,1)S(1)} %add_convert_fusion.x_ref, f32[64,16,128]{2,1,0:T(8,128)S(1)} %get-tuple-element.74.table_ref, f32[4,2048]{1,0:T(4,128)S(1)} %get-tuple-element.86.vec_ref, ...), custom_call_target="tpu_custom_call" | custom-call | flops 83886080 | bytes 6291456 | tf_op jit(solution)/shard_map/mix_attend/pallas_call | solution.py:133
  174.0 0.0 copy-start.4
  174.0 1.0 copy-done.4
  175.0 45.0 %all-gather.16.cloned.1.call-done = bf16[1,2048,2048]{2,1,0:T(8,128)(2,1)} async-done(((bf16[1,64,2048]{2,1,0:T(8,128)(2,1)}), bf16[1,2048,2048]{2,1,0:T(8,128)(2,1)}) %all-gather.16.cloned.1.call-update) | async-done | bytes 8388624 | tf_op jit(solution)/shard_map/all_gather | solution.py:178
  220.0 6.1 %fusion.17.x_ref = bf16[256,2048]{1,0:T(8,128)(2,1)S(1)} fusion(bf16[256,2048]{1,0:T(8,128)(2,1)} %copy-done.4, bf16[1,2048,2048]{2,1,0:T(8,128)(2,1)} %all-gather.16.cloned.1.call-done, bf16[256,2048]{1,0:T(8,128)(2,1)S(1)} %get-tuple-element.66), kind=kOutput, calls=%fused_computation.11 | convolution fusion | flops 2149056512 | bytes 11534336 | tf_op jit(solution)/shard_map/dot_general | solution.py:203
  226.1 26.9 %mix_attend.6 = (bf16[256,2048]{1,0:T(8,128)(2,1)S(1)}, bf16[256,2048]{1,0:T(8,128)(2,1)S(1)}) custom-call(f32[256]{0:T(256)S(1)} %add_convert_fusion.1.keep_ref, bf16[256,2048]{1,0:T(8,128)(2,1)S(1)} %fusion.17.x_ref, f32[64,16,128]{2,1,0:T(8,128)S(1)} %get-tuple-element.73.table_ref, f32[4,2048]{1,0:T(4,128)S(1)} %get-tuple-element.85.vec_ref, ...), custom_call_target="tpu_custom_call" | custom-call | flops 83886080 | bytes 6291456 | tf_op jit(solution)/shard_map/mix_attend/pallas_call | solution.py:133
  253.0 46.0 %all-gather.18.cloned.1.call-done = bf16[1,2048,2048]{2,1,0:T(8,128)(2,1)} async-done(((bf16[1,64,2048]{2,1,0:T(8,128)(2,1)}), bf16[1,2048,2048]{2,1,0:T(8,128)(2,1)}) %all-gather.18.cloned.1.call-update) | async-done | bytes 8388624 | tf_op jit(solution)/shard_map/all_gather | solution.py:178
  299.1 5.8 %fusion.14.x_ref = bf16[256,2048]{1,0:T(8,128)(2,1)S(1)} fusion(bf16[256,2048]{1,0:T(8,128)(2,1)S(1)} %get-tuple-element.69, bf16[1,2048,2048]{2,1,0:T(8,128)(2,1)} %all-gather.18.cloned.1.call-done, bf16[256,2048]{1,0:T(8,128)(2,1)S(1)} %get-tuple-element.68), kind=kOutput, calls=%fused_computation.10 | convolution fusion | flops 2149056512 | bytes 11534336 | tf_op jit(solution)/shard_map/dot_general | solution.py:203
  304.8 26.9 %mix_attend.7 = (bf16[256,2048]{1,0:T(8,128)(2,1)S(1)}, bf16[256,2048]{1,0:T(8,128)(2,1)S(1)}) custom-call(f32[256]{0:T(256)S(1)} %add_convert_fusion.1.keep_ref, bf16[256,2048]{1,0:T(8,128)(2,1)S(1)} %fusion.14.x_ref, f32[64,16,128]{2,1,0:T(8,128)S(1)} %get-tuple-element.72.table_ref, f32[4,2048]{1,0:T(4,128)S(1)} %get-tuple-element.84.vec_ref, ...), custom_call_target="tpu_custom_call" | custom-call | flops 83886080 | bytes 6291456 | tf_op jit(solution)/shard_map/mix_attend/pallas_call | solution.py:133
  331.7 0.0 copy-start.1
  331.7 1.0 copy-done.1
  332.7 45.2 %all-gather.20.cloned.1.call-done = bf16[1,2048,2048]{2,1,0:T(8,128)(2,1)} async-done(((bf16[1,64,2048]{2,1,0:T(8,128)(2,1)}), bf16[1,2048,2048]{2,1,0:T(8,128)(2,1)}) %all-gather.20.cloned.1.call-update) | async-done | bytes 8388624 | tf_op jit(solution)/shard_map/all_gather | solution.py:178
  377.9 5.5 %fusion.26 = bf16[1,128,2048]{2,1,0:T(8,128)(2,1)} fusion(bf16[1,2048,2048]{2,1,0:T(8,128)(2,1)} %all-gather.20.cloned.1.call-done, bf16[256,2048]{1,0:T(8,128)(2,1)S(1)} %get-tuple-element.71, bf16[256,2048]{1,0:T(8,128)(2,1)} %copy-done.1), kind=kOutput, calls=%fused_computation.14 | convolution fusion | flops 1074528256 | bytes 9961472 | tf_op jit(solution)/shard_map/dot_general | solution.py:203
  (17 shorter events, 0.3 us)
Async XLA Ops:
  6.5 37.6 %copy-start = (s32[4,32]{1,0:T(4,128)S(1)}, s32[4,32]{1,0:T(4,128)}, u32[]{:S(2)}) copy-start(s32[4,32]{1,0:T(4,128)} %param.36) | copy-start | bytes 1540
  6.5 30.2 %copy-start.8 = (s32[24,4]{0,1:T(4,128)S(1)}, s32[24,4]{0,1:T(4,128)}, u32[]{:S(2)}) copy-start(s32[24,4]{0,1:T(4,128)} %constant.47.clone) | copy-start | bytes 1156
  6.5 30.3 %copy-start.9 = (s32[4]{0:T(128)S(1)}, s32[4]{0:T(128)}, u32[]{:S(2)}) copy-start(s32[4]{0:T(128)} %param.37) | copy-start | bytes 52
  6.5 31.6 %copy-start.10 = (bf16[1,128,2048]{2,1,0:T(8,128)(2,1)S(1)}, bf16[1,128,2048]{2,1,0:T(8,128)(2,1)}, u32[]{:S(2)}) copy-start(bf16[1,128,2048]{2,1,0:T(8,128)(2,1)} %param.35) | copy-start | bytes 1572868
  6.5 38.1 %copy-start.5 = (f32[1,2,2048]{2,1,0:T(2,128)S(1)}, f32[1,2,2048]{2,1,0:T(2,128)}, u32[]{:S(2)}) copy-start(f32[1,2,2048]{2,1,0:T(2,128)} %param.43) | copy-start | bytes 49156
  6.5 38.1 %copy-start.7 = (f32[1,2048]{1,0:T(1,128)S(1)}, f32[1,2048]{1,0:T(1,128)}, u32[]{:S(2)}) copy-start(f32[1,2048]{1,0:T(1,128)} %param.38) | copy-start | bytes 24580
  6.6 38.1 %copy-start.6 = (f32[1,2048]{1,0:T(1,128)S(1)}, f32[1,2048]{1,0:T(1,128)}, u32[]{:S(2)}) copy-start(f32[1,2048]{1,0:T(1,128)} %param.42) | copy-start | bytes 24580
  6.6 70.8 %all-gather.12.cloned.1.call-start = ((), (), s32[]{:S(2)}) async-start(), calls=%async_computation.1 | async-start | bytes 2621440 | tf_op jit(solution)/shard_map/all_gather | solution.py:184
  10.2 130.7 %all-gather.14.cloned.1.call-start = ((), (), s32[]{:S(2)}) async-start(), calls=%async_computation.2 | async-start | bytes 8650752 | tf_op jit(solution)/shard_map/all_gather | solution.py:178
  34.9 185.2 %all-gather.16.cloned.1.call-start = ((), (), s32[]{:S(2)}) async-start(), calls=%async_computation.3 | async-start | bytes 8650752 | tf_op jit(solution)/shard_map/all_gather | solution.py:178
  35.6 263.4 %all-gather.18.cloned.1.call-start = ((), (), s32[]{:S(2)}) async-start(), calls=%async_computation.4 | async-start | bytes 8650752 | tf_op jit(solution)/shard_map/all_gather | solution.py:178
  36.2 341.7 %all-gather.20.cloned.1.call-start = ((), (), s32[]{:S(2)}) async-start(), calls=%async_computation.5 | async-start | bytes 8650752 | tf_op jit(solution)/shard_map/all_gather | solution.py:178
  38.2 1.4 collective-permute-start.5
  39.7 36.5 %collective-permute-start.24 = (bf16[128,2048]{1,0:T(8,128)(2,1)}, bf16[128,2048]{1,0:T(8,128)(2,1)S(1)}, u32[]{:S(2)}, u32[]{:S(2)}) collective-permute-start(bf16[128,2048]{1,0:T(8,128)(2,1)} %get-tuple-element.92), channel_id=1, source_target_pairs={{0,1},{1,2},{2,3},{3,4},{4,5},{5,6},{6,7},{8,9},{9,10},{10,11},{11... | collective-permute-start | bytes 1572872 | tf_op jit(solution)/shard_map/ppermute | solution.py:188
  105.9 1.0 copy-start.2
  106.9 1.0 copy-start.3
  174.0 1.0 copy-start.4
  331.7 1.0 copy-start.1
Sparse Core Ops, SparseCore 0:
  10.3 42.0 all-gather.11
  55.3 85.5 all-gather.13
  143.8 76.2 all-gather.15
  222.8 76.2 all-gather.17
  301.8 76.0 all-gather.19
